TPU v7x, 256 devices: a whole 4x4x8 slice. The times are simulated.
256 devices in a mesh: req: 32 (over x, z), tp: 8 (over y, core).
Axes of the slice: x: 4, y: 4, z: 8, core: 2. Of those that a mesh axis runs over, the one named last changes fastest.
Arguments:
- hidden_in: bfloat16 [32, 1024, 1024], P('req', 'tp'), may hold values from -6 to 6
- short_cache: bfloat16 [32, 1536, 2, 1024], P('req', None, None, 'tp')
- long_cache: bfloat16 [3, 16384, 2, 1024], P(None, 'req', None, 'tp')
- short_len: int32 [32], P('req'), may hold values from 512 to 1536, as said below
- long_owner: int32 [3], replicated, may hold values from 0 to 31, as said below
- w_qkv: bfloat16 [3, 1024, 1024], P(None, None, 'tp'), may hold values from -0.1875 to 0.1875
- b_qkv: float32 [3, 1024], P(None, 'tp'), may hold values from -3 to 3
- w_out: bfloat16 [1024, 1024], P('tp'), may hold values from -0.1875 to 0.1875
- b_out: float32 [1024], replicated, may hold values from -3 to 3
- w_in: bfloat16 [1024, 4096], P(None, 'tp'), may hold values from -0.1875 to 0.1875
- b_in: float32 [4096], P('tp'), may hold values from -3 to 3
- w_down: bfloat16 [4096, 1024], P('tp'), may hold values from -0.09375 to 0.09375
- b_down: float32 [1024], replicated, may hold values from -3 to 3
- norm_gain: float32 [2, 1024], replicated, may hold values from 0.1 to 1.9
- norm_offset: float32 [2, 1024], replicated, may hold values from -2 to 2
Outputs:
- hidden_out: bfloat16 [32, 1024, 1024], P('req', 'tp')
- new_kv: bfloat16 [32, 1024, 2, 1024], P('req', None, None, 'tp')
Inputs may be any that keep to these rules, and one draw needn't show every extreme that they name: `short_len`: some request uses all 1536 positions. `long_owner`: 3 different requests.
All inputs are finite; a program needn't handle non-finite values.
Results may differ from a plain program's by a relative error of at most 0.025.
The roundings to bfloat16 on the way count: a program that leaves them out, or rounds other values in their place, can miss the bound.
Values may be sent and summed in bfloat16 or wider, within the bound.
A program may use at most 192 MiB of HBM per device.

v0:
```python
import jax
import jax.numpy as jnp
from jax import lax
from jax.sharding import PartitionSpec as P

HEAD_DIM = 64


masked_score = -1e30


def layer_norm(rows_in, gain, shift):
    center = rows_in - jnp.mean(rows_in, axis=-1, keepdims=True)
    spread = jnp.mean(center * center, axis=-1, keepdims=True)
    return center * lax.rsqrt(spread + 1e-05) * gain + shift


def partial_attend(query_matrix, key_matrix, value_matrix, allowed):
    logit_scores = jnp.einsum(
        "wux,jux->uwj", query_matrix, key_matrix, preferred_element_type=jnp.float32
    )
    logit_scores = jnp.where(allowed[None], logit_scores, masked_score)
    row_peak = jnp.max(logit_scores, axis=2)
    softmax_weights = jnp.where(allowed[None], jnp.exp(logit_scores - row_peak[:, :, None]), 0.0)
    row_total = jnp.sum(softmax_weights, axis=2)
    summed = jnp.einsum(
        "rij,jrx->irx",
        softmax_weights.astype(jnp.bfloat16),
        value_matrix,
        preferred_element_type=jnp.float32,
    )
    return (row_peak, row_total, summed.reshape(summed.shape[0], -1))


def merge_parts(first, second):
    joint_peak = jnp.maximum(first[0], second[0])
    first_scale = jnp.exp(first[0] - joint_peak)
    second_scale = jnp.exp(second[0] - joint_peak)
    joint_total = first[1] * first_scale + second[1] * second_scale
    first_wide = jnp.repeat(jnp.swapaxes(first_scale, -1, -2), HEAD_DIM, axis=-1)
    second_wide = jnp.repeat(jnp.swapaxes(second_scale, -1, -2), HEAD_DIM, axis=-1)
    return (joint_peak, joint_total, first[2] * first_wide + second[2] * second_wide)


def empty_part(head_count, row_count):
    return (
        jnp.full((head_count, row_count), masked_score, jnp.float32),
        jnp.zeros((head_count, row_count), jnp.float32),
        jnp.zeros((row_count, head_count * HEAD_DIM), jnp.float32),
    )


def attend_long(query_matrix, cache_rows):
    head_count = query_matrix.shape[1]
    block_len = min(1024, cache_rows.shape[0])
    block_count = cache_rows.shape[0] // block_len
    blocks = cache_rows.reshape(block_count, block_len, 2, head_count, HEAD_DIM)

    def fold_block(carry, piece):
        allowed = jnp.ones((1, block_len), bool)
        return (
            merge_parts(carry, partial_attend(query_matrix, piece[:, 0], piece[:, 1], allowed)),
            None,
        )

    result, unused = lax.scan(fold_block, empty_part(head_count, query_matrix.shape[0]), blocks)
    return result


def body(
    hidden_in,
    short_cache,
    long_cache,
    short_len,
    long_owner,
    w_qkv,
    b_qkv,
    w_out,
    b_out,
    w_in,
    b_in,
    w_down,
    b_down,
    norm_gain,
    norm_offset,
):
    local_rows = hidden_in[0]
    factors = jnp.array([0.125, 1.0, 1.0], jnp.float32)[None, :, None]
    mixed = jnp.einsum(
        "nd,cdk->nck",
        lax.all_gather(local_rows, "tp", axis=0, tiled=True),
        w_qkv,
        preferred_element_type=jnp.float32,
    )
    projected = ((mixed + b_qkv[None]) * factors).astype(jnp.bfloat16)
    span_len = projected.shape[0]
    head_count = projected.shape[2] // HEAD_DIM
    flat_queries = projected[:, 0]
    query_matrix = flat_queries.reshape(span_len, head_count, HEAD_DIM)
    new_keys = projected[:, 1].reshape(span_len, head_count, HEAD_DIM)
    new_values = projected[:, 2].reshape(span_len, head_count, HEAD_DIM)
    new_kv = projected[None, :, 1:3]
    short_rows = short_cache[0]
    cache_len = short_rows.shape[0]
    all_keys = jnp.concatenate(
        [short_rows[:, 0].reshape(cache_len, head_count, HEAD_DIM), new_keys], axis=0
    )
    all_values = jnp.concatenate(
        [short_rows[:, 1].reshape(cache_len, head_count, HEAD_DIM), new_values], axis=0
    )
    cache_mask = jnp.arange(cache_len) < short_len[0]
    query_block = min(512, span_len)
    block_count = span_len // query_block

    def local_block(block_index):
        first_row = block_index * query_block
        block_queries = lax.dynamic_slice_in_dim(query_matrix, first_row, query_block, 0)
        row_ids = first_row + jnp.arange(query_block)
        causal = jnp.arange(span_len)[None, :] <= row_ids[:, None]
        allowed = jnp.concatenate(
            [jnp.broadcast_to(cache_mask[None], (query_block, cache_len)), causal], axis=1
        )
        return partial_attend(block_queries, all_keys, all_values, allowed)

    block_peak, block_total, block_sums = lax.map(local_block, jnp.arange(block_count))
    resident_portion = (
        jnp.moveaxis(block_peak, 0, 1).reshape(head_count, span_len),
        jnp.moveaxis(block_total, 0, 1).reshape(head_count, span_len),
        block_sums.reshape(span_len, -1),
    )
    my_request = lax.axis_index("req")
    owned = long_owner == my_request
    has_long = jnp.any(owned)
    which_long = jnp.sum(jnp.where(owned, jnp.arange(owned.shape[0], dtype=jnp.int32), 0))
    stripes = lax.all_gather(long_cache, "req", axis=1, tiled=True)
    chosen = lax.dynamic_index_in_dim(stripes, which_long, 0, keepdims=False)
    long_part = lax.cond(
        has_long,
        lambda rows_given: attend_long(query_matrix, rows_given),
        lambda rows_given: empty_part(head_count, span_len),
        chosen,
    )
    whole = merge_parts(resident_portion, long_part)
    context = (whole[2] / jnp.repeat(whole[1].T, HEAD_DIM, axis=1)).astype(jnp.bfloat16)
    attended = (
        lax.psum_scatter(
            jnp.dot(context, w_out, preferred_element_type=jnp.float32),
            "tp",
            scatter_dimension=0,
            tiled=True,
        )
        + b_out
    )
    normed = layer_norm(
        local_rows.astype(jnp.float32) + attended, norm_gain[0], norm_offset[0]
    ).astype(jnp.bfloat16)
    units = jax.nn.gelu(
        jnp.dot(
            lax.all_gather(normed, "tp", axis=0, tiled=True),
            w_in,
            preferred_element_type=jnp.float32,
        )
        + b_in,
        approximate=False,
    ).astype(jnp.bfloat16)
    mixed = (
        lax.psum_scatter(
            jnp.dot(units, w_down, preferred_element_type=jnp.float32),
            "tp",
            scatter_dimension=0,
            tiled=True,
        )
        + b_down
    )
    hidden_out = layer_norm(
        normed.astype(jnp.float32) + mixed, norm_gain[1], norm_offset[1]
    ).astype(jnp.bfloat16)
    return (hidden_out[None], new_kv)


def solution(mesh):
    return jax.shard_map(
        body,
        mesh=mesh,
        in_specs=(
            P("req", "tp", None),
            P("req", None, None, "tp"),
            P(None, "req", None, "tp"),
            P("req"),
            P(),
            P(None, None, "tp"),
            P(None, "tp"),
            P("tp", None),
            P(),
            P(None, "tp"),
            P("tp"),
            P("tp", None),
            P(),
            P(),
            P(),
        ),
        out_specs=(P("req", "tp", None), P("req", None, None, "tp")),
        check_vma=False,
    )
```

profile of v0, /device:TPU:6, one launch (start us, length us, event | category | flops | bytes accessed | tf_op | source)
XLA Modules:
  0.0 645.5 jit_solution(10705610684376812203)
XLA Ops:
  8.0 3.0 copy.41
  11.1 1.2 fusion.114
  13.0 1.2 copy.37
  14.1 1.1 fusion.115
  15.3 1.7 copy.38
  17.5 23.1 %all-gather.9.cloned.1.call-done = bf16[1,1024,1024]{2,1,0:T(8,128)(2,1)} async-done(((bf16[1,128,1024]{2,1,0:T(8,128)(2,1)}), bf16[1,1024,1024]{2,1,0:T(8,128)(2,1)}) %all-gather.9.cloned.1.call-update) | async-done | bytes 2097168 | tf_op jit(solution)/shard_map/all_gather | solution.py:91
  40.6 2.6 fusion.32
  45.9 24.4 %while.40 = (s32[]{:T(128)}, f32[2,2,512]{2,1,0:T(2,128)S(1)}, f32[2,2,512]{2,1,0:T(2,128)S(1)}, f32[2,512,128]{2,1,0:T(8,128)}, s32[2]{0:T(128)}, /*index=5*/bf...) while((s32[]{:T(128)}, f32[2,2,512]{2,1,0:T(2,128)S(1)}, ...), condition=%wide.region_3.4_spmd.clone, body=%wide.region_0.3_spmd.clone.sunk | while | flops 699138048 | bytes 43167992 | solution.py:125
  45.9 1.3 dynamic_slice.33
  49.5 2.0 select_reduce_fusion.3
  51.5 3.2 fusion.143
  54.8 2.5 fusion.144
  58.1 1.3 dynamic_slice.33
  61.7 2.0 select_reduce_fusion.3
  63.7 3.2 fusion.143
  67.0 2.5 fusion.144
  70.3 169.1 %all-gather.5.cloned.1.call-done = bf16[3,16384,2,128]{1,3,2,0:T(8,128)(2,1)} async-done(((bf16[3,512,2,128]{1,3,2,0:T(8,128)(2,1)}), bf16[3,16384,2,128]{1,3,2,0:T(8,128)(2,1)}) %all-gather.5.cloned.1.call-update) | async-done | bytes 25165840 | tf_op jit(solution)/shard_map/all_gather | solution.py:135
  239.4 1.5 conditional.1
  242.4 1.3 fusion.75
  243.8 2.7 fusion.119
  247.1 306.0 %reduce-scatter.3.cloned.1.call-done = f32[128,1024]{1,0:T(8,128)} async-done(((f32[1024,1024]{1,0:T(8,128)}), f32[128,1024]{1,0:T(8,128)}) %reduce-scatter.3.cloned.1.call-update) | async-done | bytes 524304 | tf_op jit(solution)/shard_map/reduce_scatter | solution.py:146
  553.2 1.2 fusion.78
  554.4 1.2 multiply_reduce_fusion.1
  555.6 1.9 add_convert_fusion.1
  557.6 26.7 %all-gather.7.cloned.1.call-done = bf16[1024,1024]{1,0:T(8,128)(2,1)} async-done(((bf16[128,1024]{1,0:T(8,128)(2,1)}), bf16[1024,1024]{1,0:T(8,128)(2,1)}) %all-gather.7.cloned.1.call-update) | async-done | bytes 2097168 | tf_op jit(solution)/shard_map/all_gather | solution.py:159
  584.4 9.3 %fusion.41 = f32[1024,1024]{1,0:T(8,128)} fusion(bf16[512,1024]{1,0:T(8,128)(2,1)S(1)} %copy-done, bf16[1024,1024]{1,0:T(8,128)(2,1)} %all-gather.7.cloned.1.call-done, bf16[1024,512]{1,0:T(8,128)(2,1)S(1)} %copy-done.20, f32[512]{0:T(512)S(1)} %copy-done.21), kind=kOutput, calls=%fused_computation.66 | convolution fusion | flops 2182086656 | bytes 8390656 | tf_op jit(solution)/shard_map/dot_general | solution.py:168
  593.7 1.1 copy-done.4
  594.9 1.1 copy.46
  596.0 38.6 %reduce-scatter.5.cloned.1.call-done = f32[128,1024]{1,0:T(8,128)} async-done(((f32[1024,1024]{1,0:T(8,128)}), f32[128,1024]{1,0:T(8,128)}) %reduce-scatter.5.cloned.1.call-update) | async-done | bytes 524304 | tf_op jit(solution)/shard_map/reduce_scatter | solution.py:167
  634.6 1.2 fusion.77
  635.8 1.2 multiply_reduce_fusion
  637.1 1.9 fusion.76
  (95 shorter events, 12.3 us)
Async XLA Ops:
  7.2 577.2 %copy-start = (bf16[512,1024]{1,0:T(8,128)(2,1)S(1)}, bf16[512,1024]{1,0:T(8,128)(2,1)}, u32[]{:S(2)}) copy-start(bf16[512,1024]{1,0:T(8,128)(2,1)} %param.33) | copy-start | bytes 3145732
  7.2 4.0 copy-start.19
  7.2 5.8 copy-start.9
  7.2 6.9 %copy-start.6 = (bf16[1,1536,2,128]{3,2,1,0:T(2,128)(2,1)S(1)}, bf16[1,1536,2,128]{3,2,1,0:T(2,128)(2,1)}, u32[]{:S(2)}) copy-start(bf16[1,1536,2,128]{3,2,1,0:T(2,128)(2,1)} %param.23) | copy-start | bytes 2359300
  7.2 33.4 %all-gather.9.cloned.1.call-start = ((), (), s32[]{:S(2)}) async-start(), calls=%async_computation.6 | async-start | bytes 2359296 | tf_op jit(solution)/shard_map/all_gather | solution.py:91
  7.9 231.4 %all-gather.5.cloned.1.call-start = ((), (), s32[]{:S(2)}) async-start(), calls=%async_computation.2 | async-start | bytes 25952256 | tf_op jit(solution)/shard_map/all_gather | solution.py:135
  11.1 542.1 %reduce-scatter.3.cloned.1.call-start = ((), (), s32[]{:S(2)}) async-start(), calls=%async_computation.3 | async-start | bytes 4718592 | tf_op jit(solution)/shard_map/reduce_scatter | solution.py:146
  15.3 25.3 %copy-start.10 = (bf16[3,1024,128]{1,2,0:T(8,128)(2,1)S(1)}, bf16[3,1024,128]{1,2,0:T(8,128)(2,1)}, u32[]{:S(2)}) copy-start(bf16[3,1024,128]{1,2,0:T(8,128)(2,1)} %copy.37) | copy-start | bytes 2359300
  40.6 2.6 copy-start.17
  40.6 2.7 copy-start.18
  43.2 1.1 copy-start.8
  43.5 0.9 copy-start.3
  51.5 3.3 copy-start.11
  63.7 3.3 copy-start.11
  240.8 1.1 copy-start.7
  242.2 1.5 copy-start.12
  246.4 0.7 copy-start.15
  246.4 0.7 copy-start.16
  246.4 306.8 %copy-start.5 = (bf16[1,128,1024]{2,1,0:T(8,128)(2,1)S(1)}, bf16[1,128,1024]{2,1,0:T(8,128)(2,1)}, u32[]{:S(2)}) copy-start(bf16[1,128,1024]{2,1,0:T(8,128)(2,1)} %param.22) | copy-start | bytes 786436
  246.4 306.8 %copy-start.13 = (f32[1024]{0:T(1024)S(1)}, f32[1024]{0:T(1024)}, u32[]{:S(2)}) copy-start(f32[1024]{0:T(1024)} %param.30) | copy-start | bytes 12292
  246.5 337.9 %copy-start.20 = (bf16[1024,512]{1,0:T(8,128)(2,1)S(1)}, bf16[1024,512]{1,0:T(8,128)(2,1)}, u32[]{:S(2)}) copy-start(bf16[1024,512]{1,0:T(8,128)(2,1)} %param.31) | copy-start | bytes 3145732
  246.5 337.9 %copy-start.21 = (f32[512]{0:T(512)S(1)}, f32[512]{0:T(512)}, u32[]{:S(2)}) copy-start(f32[512]{0:T(512)} %param.32) | copy-start | bytes 6148
  246.5 337.9 %all-gather.7.cloned.1.call-start = ((), (), s32[]{:S(2)}) async-start(), calls=%async_computation.4 | async-start | bytes 2359296 | tf_op jit(solution)/shard_map/all_gather | solution.py:159
  557.6 77.1 %reduce-scatter.5.cloned.1.call-start = ((), (), s32[]{:S(2)}) async-start(), calls=%async_computation.5 | async-start | bytes 4718592 | tf_op jit(solution)/shard_map/reduce_scatter | solution.py:167
  593.7 1.1 copy-start.4
  594.8 39.8 %copy-start.2 = (bf16[128,1024]{1,0:T(8,128)(2,1)S(1)}, bf16[128,1024]{1,0:T(8,128)(2,1)}, u32[]{:S(2)}) copy-start(bf16[128,1024]{1,0:T(8,128)(2,1)} %add_convert_fusion.1) | copy-start | bytes 786436
  594.8 39.8 %copy-start.14 = (f32[1024]{0:T(1024)S(1)}, f32[1024]{0:T(1024)}, u32[]{:S(2)}) copy-start(f32[1024]{0:T(1024)} %param.34) | copy-start | bytes 12292
Sparse Core Ops, SparseCore 0:
  9.9 30.6 all-gather.8
  43.0 196.2 all-gather.4
  246.6 306.5 reduce-scatter.2
  557.7 26.6 all-gather.6
  593.9 40.7 reduce-scatter.4
where the time goes:
time: 649 us; the launch traced here: 646 us
  waiting for transfers between devices  564 us (87%)
  matrix products  23.6 us (4%)
  other arithmetic  22.7 us (3%)
  local copies, waits for them, and re-layouts  18.2 us (3%)
  between operations  14.7 us (2%)
    reduce_scatter x1, waiting for transfers between devices, body(): lax.psum_scatter(jnp.dot(context, w_out, preferred_element_type=jnp.float...  306 us
    all_gather x1, waiting for transfers between devices, body(): stripes = lax.all_gather(long_cache, 'req', axis=1, tiled=True)  169 us
    reduce_scatter x1, waiting for transfers between devices, body(): lax.psum_scatter(jnp.dot(units, w_down, preferred_element_type=jnp.float3...  38.6 us
    all_gather x1, waiting for transfers between devices, body(): lax.all_gather(normed, 'tp', axis=0, tiled=True)  26.7 us
    all_gather x1, waiting for transfers between devices, body(): lax.all_gather(local_rows, 'tp', axis=0, tiled=True)  23.1 us
  transfers between devices with their start and end apart: 5, of which 5 were waited for; matrix products, arithmetic and copies ran while one was open for 6% of the time, Pallas kernels for 0%

commit v1 on v0

v1 whole, which is shorter than its diff:
```python
import jax
import jax.numpy as jnp
from jax import lax
from jax.experimental import pallas as pl
from jax.experimental.pallas import tpu as pltpu
from jax.sharding import PartitionSpec as P

MESH = pl.DeviceIdType.MESH
F32 = jnp.float32
BF16 = jnp.bfloat16
LOW = -1e30

NREQ, NX, NZ = 32, 4, 8
NTP, NY = 8, 4
SPAN, D, WIDE = 1024, 1024, 128
SHORT, LSEG, NLONG = 1536, 512, 3
CH = 32
MSG = 48
FFH = 512


def dot(a, b):
    return jnp.dot(a, b, preferred_element_type=F32)


def dot_t(a, b):
    return lax.dot_general(a, b, (((1,), (1,)), ((), ())), preferred_element_type=F32)


def rows_of(block, size, count=None):
    return pl.ds(pl.multiple_of(block * size, size), count or size)


def kernel(
    hid_hbm, short_hbm, long_hbm, short_len, owner, wqkv_hbm, b_qkv, wout_hbm, b_out,
    win_hbm, bin_hbm, wdown_hbm, b_down, gain, offset,
    out_ref, newkv_hbm,
    hid, wq, short_raw, long_raw, wo, w1, w2, b1, q_s, k_s, v_s, kl, vl, qa, sel, qz, bias,
    spread, weave, m_st, o_st, m_l, l_l, o_l, ps, pr, merged, rs, rr, ctx, cr, nrm, part,
    own_sum, ra, rb, fl, fr, kvout,
    s_loc, s_hs, s_hr, s_ws, s_wr, s_xs, s_xr, s_es, s_er, s_qas, s_qar, s_qzs, s_qzr,
    s_ps, s_pr, s_rs, s_rr, s_cs, s_cr, s_ns, s_nr, s_fs, s_fr, s_out,
):
    me_r, me_t = lax.axis_index("req"), lax.axis_index("tp")
    y, c = me_t // 2, me_t % 2
    x, z = me_r // NZ, me_r % NZ
    yl, yr, yf = (y + 3) % 4, (y + 1) % 4, (y + 2) % 4
    right, left = (me_r, yr * 2 + c), (me_r, yl * 2 + c)
    sibling = (me_r, y * 2 + 1 - c)
    x_right, x_left = (((x + 1) % 4) * NZ + z, me_t), (((x + 3) % 4) * NZ + z, me_t)

    def remote(src, dst, ss, rs_, dev):
        return pltpu.make_async_remote_copy(
            src_ref=src, dst_ref=dst, send_sem=ss, recv_sem=rs_, device_id=dev, device_id_type=MESH
        )

    def await_bytes(ref, sem):
        pltpu.make_async_copy(ref, ref, sem).wait()

    loads = [
        (hid_hbm, hid.at[me_t]),
        (long_hbm, long_raw.at[0]),
        (short_hbm, short_raw),
        (wqkv_hbm.at[0], wq.at[:, pl.ds(0, WIDE)]),
        (wqkv_hbm.at[1], wq.at[:, pl.ds(WIDE, WIDE)]),
        (wqkv_hbm.at[2], wq.at[:, pl.ds(2 * WIDE, WIDE)]),
        (wout_hbm, wo.at[me_t]),
        (win_hbm, w1.at[c]),
        (wdown_hbm, w2.at[c]),
        (bin_hbm, b1.at[c]),
    ]
    loads = [pltpu.make_async_copy(s, d, s_loc.at[i]) for i, (s, d) in enumerate(loads)]
    for load in loads:
        load.start()

    barrier = pltpu.get_barrier_semaphore()

    @pl.loop(1, NREQ)
    def _(d):
        pl.semaphore_signal(barrier, inc=1, device_id=((me_r + d) % NREQ, me_t), device_id_type=MESH)

    @pl.loop(1, NTP)
    def _(d):
        pl.semaphore_signal(barrier, inc=1, device_id=(me_r, (me_t + d) % NTP), device_id_type=MESH)

    pl.semaphore_wait(barrier, NREQ - 1 + NTP - 1)

    def gather_start(buf, ss, sr):
        mine = buf.at[me_t]
        copies = [
            remote(mine, mine, ss.at[1], sr.at[0], right),
            remote(mine, mine, ss.at[2], sr.at[1], left),
            remote(mine, mine, ss.at[0], sr.at[4], sibling),
        ]
        for copy in copies:
            copy.start()
        return copies

    def gather_step(buf, ss, sr, step):
        if step == 1:
            slot = yl * 2 + c
            await_bytes(buf.at[slot], sr.at[0])
            half = buf.at[slot, pl.ds(0, 64)]
            copies = [
                remote(half, half, ss.at[3], sr.at[2], right),
                remote(buf.at[slot], buf.at[slot], ss.at[4], sr.at[5], sibling),
            ]
        elif step == 2:
            slot = yr * 2 + c
            await_bytes(buf.at[slot], sr.at[1])
            half = buf.at[slot, pl.ds(64, 64)]
            copies = [
                remote(half, half, ss.at[5], sr.at[3], left),
                remote(buf.at[slot], buf.at[slot], ss.at[6], sr.at[6], sibling),
            ]
        else:
            slot = yf * 2 + c
            await_bytes(buf.at[slot, pl.ds(0, 64)], sr.at[2])
            await_bytes(buf.at[slot, pl.ds(64, 64)], sr.at[3])
            copies = [remote(buf.at[slot], buf.at[slot], ss.at[7], sr.at[7], sibling)]
        for copy in copies:
            copy.start()
        return copies

    def gather_sibling(buf, sr, step):
        slot = (y, yl, yr, yf)[step] * 2 + 1 - c
        await_bytes(buf.at[slot], sr.at[4 + step])

    sent = []
    loads[0].wait()
    sent += gather_start(hid, s_hs, s_hr)
    loads[1].wait()
    x_copies = [
        remote(long_raw.at[0], long_raw.at[1], s_xs.at[0], s_xr.at[0], x_right),
        remote(long_raw.at[0], long_raw.at[2], s_xs.at[1], s_xr.at[1], x_left),
    ]
    for copy in x_copies:
        copy.start()
    sent += x_copies

    row256 = lax.broadcasted_iota(jnp.int32, (256, 256), 0)
    col256 = lax.broadcasted_iota(jnp.int32, (256, 256), 1)
    target = jnp.where(row256 < 128, 2 * row256, 2 * (row256 - 128) + 1)
    spread[...] = jnp.where(col256 == target, 1.0, 0.0).astype(BF16)
    target_t = jnp.where(col256 < 128, 2 * col256, 2 * (col256 - 128) + 1)
    weave[...] = jnp.where(row256 == target_t, 1.0, 0.0).astype(BF16)
    bias[...] = jnp.where(
        lax.broadcasted_iota(jnp.int32, (8, SHORT), 1) < short_len[0], 0.0, LOW
    )
    lane = lax.broadcasted_iota(jnp.int32, (1, WIDE), 1)
    first = jnp.where(lane < 64, 1.0, 0.0).astype(BF16)
    second = jnp.where(lane < 64, 0.0, 1.0).astype(BF16)

    def unweave(tile):
        both = dot(spread[...], tile).astype(BF16)
        return both[:128], both[128:]

    loads[2].wait()

    @pl.loop(0, 3)
    def _(g):
        for i in range(4):
            at = g * 4 + i
            keys, values = unweave(short_raw[rows_of(at, 256), :])
            k_s[rows_of(at, 128), :] = keys
            v_s[rows_of(at, 128), :] = values

    def unweave_long(slot):
        @pl.loop(0, NLONG)
        def _(j):
            for i in range(4):
                keys, values = unweave(long_raw[slot, rows_of(j * 4 + i, 256), :])
                kl[j * 4 + slot, pl.ds(i * 128, 128), :] = keys
                vl[j * 4 + slot, pl.ds(i * 128, 128), :] = values

    for i in (3, 4, 5):
        loads[i].wait()

    def project(t):
        mixed = dot(hid[t], wq[...])
        q = ((mixed[:, :WIDE] + b_qkv[0:1, :]) * 0.125).astype(BF16)
        k = (mixed[:, WIDE : 2 * WIDE] + b_qkv[1:2, :]).astype(BF16)
        v = (mixed[:, 2 * WIDE :] + b_qkv[2:3, :]).astype(BF16)
        q_s[rows_of(t, 128), :] = q
        k_s[pl.ds(pl.multiple_of(SHORT + t * 128, 128), 128), :] = k
        v_s[pl.ds(pl.multiple_of(SHORT + t * 128, 128), 128), :] = v

        @pl.loop(0, 4)
        def _(i):
            to = 4 * t + i

            @pl.when(to != me_r)
            def _():
                remote(q_s.at[rows_of(to, CH), :], qa.at[me_r], s_qas, s_qar, (to, me_t)).start()

            @pl.when(to == me_r)
            def _():
                qa[me_r] = q_s[rows_of(to, CH), :]

    project(me_t)
    gather_sibling(hid, s_hr, 0)
    project(y * 2 + 1 - c)
    unweave_long(0)
    for step, yy in ((1, yl), (2, yr), (3, yf)):
        sent += gather_step(hid, s_hs, s_hr, step)
        project(yy * 2 + c)
    for step, yy in ((1, yl), (2, yr), (3, yf)):
        gather_sibling(hid, s_hr, step)
        project(yy * 2 + 1 - c)

    for i in (6, 7, 8, 9):
        loads[i].wait()
    sent += gather_start(wo, s_ws, s_wr)
    swap = [
        remote(w1.at[c], w1.at[c], s_es.at[0], s_er.at[0], sibling),
        remote(w2.at[c], w2.at[c], s_es.at[1], s_er.at[1], sibling),
        remote(b1.at[c], b1.at[c], s_es.at[2], s_er.at[2], sibling),
    ]
    for copy in swap:
        copy.start()
    sent += swap

    def attend_init():
        m_st[...] = jnp.full(m_st.shape, LOW, F32)
        o_st[...] = jnp.zeros(o_st.shape, F32)

    def attend_step(q, k, v, extra):
        vs = (v * first + second, v * second + first)
        for h, mask in enumerate((first, second)):
            s = dot_t(q * mask, k)
            if extra is not None:
                s = s + extra
            m_old = m_st[h]
            m_new = jnp.maximum(m_old, jnp.max(s, axis=1, keepdims=True))
            wide = jnp.concatenate([m_new] * (s.shape[1] // WIDE), axis=1)
            p = jnp.exp(s - wide).astype(BF16)
            o_st[h] = o_st[h] * jnp.exp(m_old - m_new) + dot(p, vs[h])
            m_st[h] = m_new

    def attend_end():
        low = lax.broadcasted_iota(jnp.int32, (256, WIDE), 1) < 64
        total = pltpu.roll(jnp.where(low, o_st[1], o_st[0]), 64, 1)
        return jnp.where(low, m_st[0], m_st[1]), total, jnp.where(low, o_st[0], o_st[1])

    def attend_local(b):
        q = q_s[rows_of(b, 256), :]
        attend_init()

        @pl.loop(0, 3)
        def _(i):
            at = rows_of(i, 512)
            attend_step(q, k_s[at, :], v_s[at, :], bias[0:1, at])

        @pl.loop(0, b)
        def _(i):
            at = pl.ds(pl.multiple_of(SHORT + i * 256, 256), 256)
            attend_step(q, k_s[at, :], v_s[at, :], None)

        at = pl.ds(pl.multiple_of(SHORT + b * 256, 256), 256)
        attend_step(q, k_s[at, :], v_s[at, :], jnp.where(col256 <= row256, 0.0, LOW))
        m, total, o = attend_end()
        m_l[rows_of(b, 256), :] = m
        l_l[rows_of(b, 256), :] = total
        o_l[rows_of(b, 256), :] = o

    lane32 = lax.broadcasted_iota(jnp.int32, (CH, WIDE), 1) % 64
    diagonal = jnp.where(lane32 == lax.broadcasted_iota(jnp.int32, (CH, WIDE), 0), 1.0, 0.0)
    tile_row = lax.broadcasted_iota(jnp.int32, (16, WIDE), 0)
    side_r = lax.broadcasted_iota(jnp.int32, (WIDE, WIDE), 0) // 64
    side_c = lax.broadcasted_iota(jnp.int32, (WIDE, WIDE), 1) // 64
    sides = jnp.where(side_r == side_c, 1.0, 0.0).astype(BF16)

    def pack_stats(lse):
        row = jnp.sum(lse * diagonal, axis=0, keepdims=True)
        hi = row.astype(BF16).astype(F32)
        mid = (row - hi).astype(BF16).astype(F32)
        lo = row - hi - mid
        tile = jnp.where(tile_row == 0, hi, jnp.where(tile_row == 1, mid, jnp.where(tile_row == 2, lo, 0.0)))
        return tile.astype(BF16)

    def unpack_stats(tiles):
        n = tiles.shape[0]
        tiles = tiles.astype(F32)
        lse = None
        for i in range(3):
            spread_out = tiles[:, i : i + 1, :] * diagonal[None]
            term = dot(spread_out.reshape(n * CH, WIDE).astype(BF16), sides)
            lse = term if lse is None else lse + term
        return lse

    @pl.loop(0, 2)
    def _(b):
        attend_local(b)

    await_bytes(qa.at[pl.ds(0, NREQ - 1)], s_qar)
    for j in range(NLONG):
        sel[j] = qa[owner[j]]
    qz[0] = sel[...]

    @pl.loop(1, NZ)
    def _(d):
        to = x * NZ + (z + d) % NZ
        remote(sel, qz.at[d], s_qzs, s_qzr, (to, me_t)).start()

    await_bytes(long_raw.at[1], s_xr.at[0])
    half = pl.ds(0, SHORT)
    copy = remote(long_raw.at[1, half], long_raw.at[3, half], s_xs.at[2], s_xr.at[2], x_right)
    copy.start()
    sent.append(copy)
    await_bytes(long_raw.at[2], s_xr.at[1])
    half = pl.ds(SHORT, SHORT)
    copy = remote(long_raw.at[2, half], long_raw.at[3, half], s_xs.at[3], s_xr.at[3], x_left)
    copy.start()
    sent.append(copy)
    for step in (1, 2):
        sent += gather_step(wo, s_ws, s_wr, step)
    unweave_long(1)
    unweave_long(2)

    attend_local(2)
    sent += gather_step(wo, s_ws, s_wr, 3)

    await_bytes(long_raw.at[3, pl.ds(0, SHORT)], s_xr.at[2])
    await_bytes(long_raw.at[3, pl.ds(SHORT, SHORT)], s_xr.at[3])
    unweave_long(3)
    await_bytes(qz.at[pl.ds(1, NZ - 1)], s_qzr)

    @pl.loop(0, NLONG)
    def _(j):
        q = qz[:, j].reshape(256, WIDE)
        attend_init()

        @pl.loop(0, NX)
        def _(i):
            attend_step(q, kl[j * 4 + i], vl[j * 4 + i], None)

        m, total, o = attend_end()
        lse = m + jnp.log(total)
        o = (o / total).astype(BF16)
        for d in range(NZ):
            at = slice(d * CH, (d + 1) * CH)
            dst = pr if d == 0 else ps
            dst[j, d, 0:CH] = o[at]
            dst[j, d, CH:MSG] = pack_stats(lse[at])

        @pl.loop(1, NZ)
        def _(d):
            to = x * NZ + (z + NZ - d) % NZ
            remote(ps.at[j, d], pr.at[j, d], s_ps.at[j], s_pr.at[j], (to, me_t)).start()

    attend_local(3)

    @pl.loop(0, NLONG)
    def _(j):
        await_bytes(pr.at[j, pl.ds(1, NZ - 1)], s_pr.at[j])
        lse = unpack_stats(pr[j, :, CH:MSG]).reshape(NZ, CH, WIDE)
        top = jnp.max(lse, axis=0, keepdims=True)
        w = jnp.exp(lse - top)
        total = jnp.sum(w, axis=0)
        o = jnp.sum(w * pr[j, :, 0:CH].astype(F32), axis=0) / total
        merged[j, 0:CH] = o
        merged[j, CH:MSG] = pack_stats(top[0] + jnp.log(total)).astype(F32)

    msg_row = lax.broadcasted_iota(jnp.int32, (MSG, WIDE), 0)
    empty = jnp.where(msg_row == CH, LOW, 0.0)

    @pl.loop(0, NREQ)
    def _(r):
        value, rest = None, 1.0
        for j in range(NLONG):
            mine = jnp.where(owner[j] == r, 1.0, 0.0)
            term = merged[j] * mine
            value = term if value is None else value + term
            rest = rest - mine
        message = (value + empty * rest).astype(BF16)

        @pl.when(r == me_r)
        def _():
            rr[me_r] = message

        @pl.when(r != me_r)
        def _():
            rs[r] = message
            remote(rs.at[r], rr.at[me_r], s_rs, s_rr, (r, me_t)).start()

    @pl.loop(0, 4)
    def _(g):
        for i in range(2):
            t = g * 2 + i
            at = pl.ds(pl.multiple_of(SHORT + t * 128, 128), 128)
            both = jnp.concatenate([k_s[at, :], v_s[at, :]], axis=0)
            kvout[rows_of(t, 256), :] = dot(weave[...], both).astype(BF16)

    out_copy = pltpu.make_async_copy(kvout, newkv_hbm, s_out.at[0])
    out_copy.start()

    await_bytes(rr.at[pl.ds(0, NREQ - 1)], s_rr)

    @pl.loop(0, 4)
    def _(b):
        at = rows_of(b, 256)
        msgs = rr[pl.ds(b * 8, 8)]
        lse = unpack_stats(msgs[:, CH:MSG])
        o = msgs[:, 0:CH].astype(F32).reshape(256, WIDE)
        m = m_l[at, :]
        top = jnp.maximum(m, lse)
        a, w = jnp.exp(m - top), jnp.exp(lse - top)
        value = (o_l[at, :] * a + o * w) / (l_l[at, :] * a + w)
        ctx[at, :] = value.astype(BF16)
        for i in range(2):
            to = b * 2 + i

            @pl.when(to != me_t)
            def _():
                remote(ctx.at[rows_of(to, 128), :], cr.at[me_t], s_cs, s_cr, (me_r, to)).start()

            @pl.when(to == me_t)
            def _():
                cr[me_t] = ctx[rows_of(to, 128), :]

    for step in range(4):
        gather_sibling(wo, s_wr, step)
    await_bytes(cr.at[pl.ds(0, NTP - 1)], s_cr)
    attended = b_out[...]
    for h in range(NTP):
        attended = attended + dot(cr[h], wo[h])

    def norm(rows, which):
        center = rows - jnp.mean(rows, axis=-1, keepdims=True)
        var = jnp.mean(center * center, axis=-1, keepdims=True)
        return (center * lax.rsqrt(var + 1e-5) * gain[which : which + 1, :] + offset[which : which + 1, :]).astype(BF16)

    nrm[0] = norm(hid[me_t].astype(F32) + attended, 0)

    copies = [
        remote(nrm.at[0], nrm.at[1], s_ns.at[0], s_nr.at[0], right),
        remote(nrm.at[0], nrm.at[2], s_ns.at[1], s_nr.at[1], left),
    ]
    for copy in copies:
        copy.start()
    sent += copies
    await_bytes(w1.at[1 - c], s_er.at[0])
    await_bytes(w2.at[1 - c], s_er.at[1])
    await_bytes(b1.at[1 - c], s_er.at[2])

    def feed(slot):
        rows = nrm[slot]
        total = None
        for i in range(2):
            u = dot(rows, w1[i]) + b1[i]
            u = (0.5 * u * (1.0 + lax.erf(u * 0.7071067811865476))).astype(BF16)
            term = dot(u, w2[i])
            total = term if total is None else total + term
        return total

    def start(*args):
        copy = remote(*args)
        copy.start()
        sent.append(copy)

    top_half, low_half = pl.ds(0, 64), pl.ds(64, 64)
    own_sum[...] = feed(0)
    await_bytes(nrm.at[1], s_nr.at[0])
    start(nrm.at[1, top_half], nrm.at[3, top_half], s_ns.at[2], s_nr.at[2], right)
    await_bytes(nrm.at[2], s_nr.at[1])
    start(nrm.at[2, low_half], nrm.at[3, low_half], s_ns.at[3], s_nr.at[3], left)
    part[1] = feed(1).astype(BF16)
    start(part.at[1, top_half], fr.at[top_half], s_fs.at[0], s_fr.at[0], left)
    part[2] = feed(2).astype(BF16)
    start(part.at[2, low_half], fl.at[low_half], s_fs.at[1], s_fr.at[1], right)
    await_bytes(nrm.at[3, top_half], s_nr.at[2])
    await_bytes(nrm.at[3, low_half], s_nr.at[3])
    part[3] = feed(3).astype(BF16)
    start(part.at[3, top_half], ra, s_fs.at[2], s_fr.at[2], right)
    start(part.at[3, low_half], rb, s_fs.at[3], s_fr.at[3], left)
    await_bytes(ra, s_fr.at[2])
    part[2, 0:64] = (part[2, 0:64].astype(F32) + ra[...].astype(F32)).astype(BF16)
    start(part.at[2, top_half], fl.at[top_half], s_fs.at[4], s_fr.at[4], right)
    await_bytes(rb, s_fr.at[3])
    part[1, 64:128] = (part[1, 64:128].astype(F32) + rb[...].astype(F32)).astype(BF16)
    start(part.at[1, low_half], fr.at[low_half], s_fs.at[5], s_fr.at[5], left)
    await_bytes(fr.at[top_half], s_fr.at[0])
    await_bytes(fl.at[low_half], s_fr.at[1])
    await_bytes(fl.at[top_half], s_fr.at[4])
    await_bytes(fr.at[low_half], s_fr.at[5])
    mixed = own_sum[...] + fl[...].astype(F32) + fr[...].astype(F32) + b_down[...]
    out_ref[...] = norm(nrm[0].astype(F32) + mixed, 1)

    for copy in sent:
        copy.wait_send()
    await_bytes(qa.at[pl.ds(0, NREQ - 1)], s_qas)
    await_bytes(qz.at[pl.ds(1, NZ - 1)], s_qzs)
    for j in range(NLONG):
        await_bytes(pr.at[j, pl.ds(1, NZ - 1)], s_ps.at[j])
    await_bytes(rr.at[pl.ds(0, NREQ - 1)], s_rs)
    await_bytes(cr.at[pl.ds(0, NTP - 1)], s_cs)
    out_copy.wait()


def body(
    hidden_in, short_cache, long_cache, short_len, long_owner, w_qkv, b_qkv, w_out, b_out,
    w_in, b_in, w_down, b_down, norm_gain, norm_offset,
):
    hbm = pl.BlockSpec(memory_space=pl.ANY)
    vmem = pl.BlockSpec(memory_space=pltpu.VMEM)
    smem = pl.BlockSpec(memory_space=pltpu.SMEM)
    V, S = pltpu.VMEM, pltpu.SemaphoreType.DMA
    hidden_out, new_kv = pl.pallas_call(
        kernel,
        out_shape=(
            jax.ShapeDtypeStruct((128, D), BF16),
            jax.ShapeDtypeStruct((2 * SPAN, WIDE), BF16),
        ),
        in_specs=[
            hbm, hbm, hbm, smem, smem, hbm, vmem, hbm, vmem, hbm, hbm, hbm, vmem, vmem, vmem,
        ],
        out_specs=(vmem, hbm),
        scratch_shapes=[
            V((NTP, 128, D), BF16),
            V((D, 3 * WIDE), BF16),
            V((2 * SHORT, WIDE), BF16),
            V((NX, 2 * NLONG * LSEG, WIDE), BF16),
            V((NTP, WIDE, D), BF16),
            V((2, D, FFH), BF16),
            V((2, FFH, D), BF16),
            V((2, 1, FFH), F32),
            V((SPAN, WIDE), BF16),
            V((SHORT + SPAN, WIDE), BF16),
            V((SHORT + SPAN, WIDE), BF16),
            V((NLONG * NX, LSEG, WIDE), BF16),
            V((NLONG * NX, LSEG, WIDE), BF16),
            V((NREQ, CH, WIDE), BF16),
            V((NLONG, CH, WIDE), BF16),
            V((NZ, NLONG, CH, WIDE), BF16),
            V((8, SHORT), F32),
            V((256, 256), BF16),
            V((256, 256), BF16),
            V((2, 256, WIDE), F32),
            V((2, 256, WIDE), F32),
            V((SPAN, WIDE), F32),
            V((SPAN, WIDE), F32),
            V((SPAN, WIDE), F32),
            V((NLONG, NZ, MSG, WIDE), BF16),
            V((NLONG, NZ, MSG, WIDE), BF16),
            V((NLONG, MSG, WIDE), F32),
            V((NREQ, MSG, WIDE), BF16),
            V((NREQ, MSG, WIDE), BF16),
            V((SPAN, WIDE), BF16),
            V((NTP, 128, WIDE), BF16),
            V((NY, 128, D), BF16),
            V((NY, 128, D), BF16),
            V((128, D), F32),
            V((64, D), BF16),
            V((64, D), BF16),
            V((128, D), BF16),
            V((128, D), BF16),
            V((2 * SPAN, WIDE), BF16),
            S((10,)), S((8,)), S((8,)), S((8,)), S((8,)), S((4,)), S((4,)), S((3,)), S((3,)),
            S, S, S, S, S((3,)), S((3,)), S, S, S, S, S((4,)), S((4,)), S((6,)), S((6,)), S((1,)),
        ],
        compiler_params=pltpu.CompilerParams(
            collective_id=0, has_side_effects=True, vmem_limit_bytes=56 * 1024 * 1024
        ),
    )(
        hidden_in[0],
        short_cache.reshape(2 * SHORT, WIDE),
        long_cache.reshape(2 * NLONG * LSEG, WIDE),
        short_len,
        long_owner,
        w_qkv,
        b_qkv,
        w_out,
        b_out[None],
        w_in,
        b_in[None],
        w_down,
        b_down[None],
        norm_gain,
        norm_offset,
    )
    return (hidden_out[None], new_kv.reshape(1, SPAN, 2, WIDE))


def solution(mesh):
    return jax.shard_map(
        body,
        mesh=mesh,
        in_specs=(
            P("req", "tp", None),
            P("req", None, None, "tp"),
            P(None, "req", None, "tp"),
            P("req"),
            P(),
            P(None, None, "tp"),
            P(None, "tp"),
            P("tp", None),
            P(),
            P(None, "tp"),
            P("tp"),
            P("tp", None),
            P(),
            P(),
            P(),
        ),
        out_specs=(P("req", "tp", None), P("req", None, None, "tp")),
        check_vma=False,
    )
```

time: 649 us -> 106 us (0.16)
  waiting for transfers between devices: 564 us -> 0 us
  Pallas kernels: 0 us -> 102 us
  matrix products: 23.6 us -> 0 us
  other arithmetic: 22.7 us -> 0 us
  local copies, waits for them, and re-layouts: 18.2 us -> 2.52 us
  between operations: 14.7 us -> 1.3 us
    reduce_scatter x2 -> x0, waiting for transfers between devices: 345 us -> none  [the longest x1 306 us: body(): lax.psum_scatter(jnp.dot(context, w_out, preferred_element_type=jnp.float...]
    all_gather x3 -> x0, waiting for transfers between devices: 219 us -> none  [the longest x1 169 us: body(): stripes = lax.all_gather(long_cache, 'req', axis=1, tiled=True)]
    pallas_call x0 -> x1, Pallas kernels: none -> 102 us  [body(): pl.pallas_call(kernel, out_shape=(jax.ShapeDtypeStruct((128, D), BF16), j...]
    dot_general x6 -> x0, matrix products: 21 us -> none  [the longest x1 9.35 us: body(): jnp.dot(units, w_down, preferred_element_type=jnp.float32)]
    reduce_sum x6 -> x0, other arithmetic: 11.4 us -> none  [the longest x2 6.49 us: partial_attend(): row_total = jnp.sum(softmax_weights, axis=2)]
  transfers between devices with their start and end apart: 5 -> 0, of which waited for: 5 -> 0; matrix products, arithmetic and copies ran while one was open for 6% -> 0% of each run, Pallas kernels for 0% -> 0%
where the time goes in v1:
time: 106 us; the launch traced here: 105 us
  Pallas kernels  102 us (96%)
  local copies, waits for them, and re-layouts  2.52 us (2%)
  between operations  1.3 us (1%)
    pallas_call x1, Pallas kernels, body(): pl.pallas_call(kernel, out_shape=(jax.ShapeDtypeStruct((128, D), BF16), j...  102 us
    unnamed x4, local copies, waits for them, and re-layouts  2.52 us

profile of v1, /device:TPU:6, one launch (start us, length us, event | category | flops | bytes accessed | tf_op | source)
XLA Modules:
  0.0 105.4 jit_solution(16580812426241269471)
XLA Ops:
  1.3 101.6 %shard_map.158 = (bf16[128,1024]{1,0:T(8,128)(2,1)}, bf16[2048,128]{1,0:T(8,128)(2,1)}) custom-call(bf16[128,1024]{1,0:T(8,128)(2,1)} %bitcast.11, bf16[3072,128]{1,0:T(8,128)(2,1)} %bitcast.8, bf16[3072,128]{1,0:T(8,128)(2,1)} %bitcast.9, s32[1]{0:T(128)S(6)} %copy.19.short_len, s32[3]{0:T(128)} %owner.1, bf16[3,1024,128]{2,1,0:T(8,128)(2,1)} %wqkv_hbm.1, ...), custom_call_target="tpu_custom_call" | custom-call | tf_op jit(solution)/shard_map/pallas_call | solution.py:508
  102.9 0.0 copy-start
  102.9 1.7 %copy.20 = bf16[1,128,1024]{2,1,0:T(8,128)(2,1)} copy(bf16[1,128,1024]{2,1,0:T(8,128)(2,1)} %bitcast.12) | data formatting | bytes 524288
  104.6 0.0 copy-done
  104.6 0.8 copy.21
Async XLA Ops:
  102.9 1.7 %copy-start = (bf16[2048,128]{1,0:T(8,128)(2,1)S(1)}, bf16[2048,128]{1,0:T(8,128)(2,1)}, u32[]{:S(2)}) copy-start(bf16[2048,128]{1,0:T(8,128)(2,1)} %get-tuple-element.5) | copy-start | bytes 1572868

commit v2 on v1

--- a/solution.py
+++ b/solution.py
@@ -36,7 +36,7 @@
     win_hbm, bin_hbm, wdown_hbm, b_down, gain, offset,
     out_ref, newkv_hbm,
     hid, wq, short_raw, long_raw, wo, w1, w2, b1, q_s, k_s, v_s, kl, vl, qa, sel, qz, bias,
-    spread, weave, m_st, o_st, m_l, l_l, o_l, ps, pr, merged, rs, rr, ctx, cr, nrm, part,
+    spread, weave, m_s, o_s, m_g, o_g, m_l, l_l, o_l, ps, pr, merged, rs, rr, ctx, cr, nrm, part,
     own_sum, ra, rb, fl, fr, kvout,
     s_loc, s_hs, s_hr, s_ws, s_wr, s_xs, s_xr, s_es, s_er, s_qas, s_qar, s_qzs, s_qzr,
     s_ps, s_pr, s_rs, s_rr, s_cs, s_cr, s_ns, s_nr, s_fs, s_fr, s_out,
@@ -47,6 +47,7 @@
     yl, yr, yf = (y + 3) % 4, (y + 1) % 4, (y + 2) % 4
     right, left = (me_r, yr * 2 + c), (me_r, yl * 2 + c)
     sibling = (me_r, y * 2 + 1 - c)
+    right_other, left_other = (me_r, yr * 2 + 1 - c), (me_r, yl * 2 + 1 - c)
     x_right, x_left = (((x + 1) % 4) * NZ + z, me_t), (((x + 3) % 4) * NZ + z, me_t)
 
     def remote(src, dst, ss, rs_, dev):
@@ -85,58 +86,77 @@
 
     pl.semaphore_wait(barrier, NREQ - 1 + NTP - 1)
 
+    top_half, low_half = pl.ds(0, 64), pl.ds(64, 64)
+
+    def begin(*args):
+        copy = remote(*args)
+        copy.start()
+        sent.append(copy)
+
     def gather_start(buf, ss, sr):
-        mine = buf.at[me_t]
-        copies = [
-            remote(mine, mine, ss.at[1], sr.at[0], right),
-            remote(mine, mine, ss.at[2], sr.at[1], left),
-            remote(mine, mine, ss.at[0], sr.at[4], sibling),
-        ]
-        for copy in copies:
-            copy.start()
-        return copies
-
-    def gather_step(buf, ss, sr, step):
+        mine, top, low = buf.at[me_t], buf.at[me_t, top_half], buf.at[me_t, low_half]
+        begin(top, top, ss.at[1], sr.at[0], right)
+        begin(low, low, ss.at[2], sr.at[2], left)
+        begin(top, top, ss.at[10], sr.at[10], right_other)
+        begin(low, low, ss.at[11], sr.at[11], left_other)
+        begin(low, low, ss.at[3], sr.at[1], right)
+        begin(top, top, ss.at[4], sr.at[3], left)
+        begin(mine, mine, ss.at[0], sr.at[6], sibling)
+
+    def gather_forward(buf, ss, sr):
+        half = buf.at[yl * 2 + c, top_half]
+        await_bytes(half, sr.at[0])
+        begin(half, half, ss.at[5], sr.at[4], right)
+        half = buf.at[yr * 2 + c, low_half]
+        await_bytes(half, sr.at[2])
+        begin(half, half, ss.at[6], sr.at[5], left)
+
+    def gather_share(buf, ss, sr, step):
+        slot = (y, yl, yr, yf)[step] * 2 + c
         if step == 1:
-            slot = yl * 2 + c
-            await_bytes(buf.at[slot], sr.at[0])
-            half = buf.at[slot, pl.ds(0, 64)]
-            copies = [
-                remote(half, half, ss.at[3], sr.at[2], right),
-                remote(buf.at[slot], buf.at[slot], ss.at[4], sr.at[5], sibling),
-            ]
+            await_bytes(buf.at[slot, low_half], sr.at[1])
         elif step == 2:
-            slot = yr * 2 + c
-            await_bytes(buf.at[slot], sr.at[1])
-            half = buf.at[slot, pl.ds(64, 64)]
-            copies = [
-                remote(half, half, ss.at[5], sr.at[3], left),
-                remote(buf.at[slot], buf.at[slot], ss.at[6], sr.at[6], sibling),
-            ]
+            await_bytes(buf.at[slot, top_half], sr.at[3])
         else:
-            slot = yf * 2 + c
-            await_bytes(buf.at[slot, pl.ds(0, 64)], sr.at[2])
-            await_bytes(buf.at[slot, pl.ds(64, 64)], sr.at[3])
-            copies = [remote(buf.at[slot], buf.at[slot], ss.at[7], sr.at[7], sibling)]
-        for copy in copies:
-            copy.start()
-        return copies
+            await_bytes(buf.at[slot, top_half], sr.at[4])
+            await_bytes(buf.at[slot, low_half], sr.at[5])
+        share = buf.at[slot] if step == 3 else buf.at[slot, (None, low_half, top_half)[step]]
+        begin(share, share, ss.at[6 + step], sr.at[6 + step], sibling)
 
     def gather_sibling(buf, sr, step):
         slot = (y, yl, yr, yf)[step] * 2 + 1 - c
-        await_bytes(buf.at[slot], sr.at[4 + step])
+        if step == 1:
+            await_bytes(buf.at[slot, top_half], sr.at[10])
+            await_bytes(buf.at[slot, low_half], sr.at[7])
+        elif step == 2:
+            await_bytes(buf.at[slot, low_half], sr.at[11])
+            await_bytes(buf.at[slot, top_half], sr.at[8])
+        else:
+            await_bytes(buf.at[slot], sr.at[6 + step])
 
     sent = []
     loads[0].wait()
-    sent += gather_start(hid, s_hs, s_hr)
+    gather_start(hid, s_hs, s_hr)
     loads[1].wait()
-    x_copies = [
-        remote(long_raw.at[0], long_raw.at[1], s_xs.at[0], s_xr.at[0], x_right),
-        remote(long_raw.at[0], long_raw.at[2], s_xs.at[1], s_xr.at[1], x_left),
-    ]
-    for copy in x_copies:
-        copy.start()
-    sent += x_copies
+
+    def x_rows(j, half=None):
+        if half is None:
+            return rows_of(j, 2 * LSEG)
+        return pl.ds(pl.multiple_of(j * 2 * LSEG + half * LSEG, LSEG), LSEG)
+
+    def x_send(j):
+        own = long_raw.at[0, x_rows(j)]
+        begin(own, long_raw.at[1, x_rows(j)], s_xs.at[4 * j], s_xr.at[4 * j], x_right)
+        begin(own, long_raw.at[2, x_rows(j)], s_xs.at[4 * j + 1], s_xr.at[4 * j + 1], x_left)
+
+    def x_forward(j):
+        for half, to in ((0, x_right), (1, x_left)):
+            await_bytes(long_raw.at[1 + half, x_rows(j)], s_xr.at[4 * j + half])
+            at, k = x_rows(j, half), 4 * j + 2 + half
+            begin(long_raw.at[1 + half, at], long_raw.at[3, at], s_xs.at[k], s_xr.at[k], to)
+
+    x_send(0)
+    x_send(1)
 
     row256 = lax.broadcasted_iota(jnp.int32, (256, 256), 0)
     col256 = lax.broadcasted_iota(jnp.int32, (256, 256), 1)
@@ -165,13 +185,12 @@
             k_s[rows_of(at, 128), :] = keys
             v_s[rows_of(at, 128), :] = values
 
-    def unweave_long(slot):
-        @pl.loop(0, NLONG)
-        def _(j):
-            for i in range(4):
-                keys, values = unweave(long_raw[slot, rows_of(j * 4 + i, 256), :])
-                kl[j * 4 + slot, pl.ds(i * 128, 128), :] = keys
-                vl[j * 4 + slot, pl.ds(i * 128, 128), :] = values
+    def unweave_long(j, slot):
+        for i in range(4):
+            keys, values = unweave(long_raw[slot, rows_of(j * 4 + i, 256), :])
+            at = pl.ds(slot * LSEG + i * 128, 128)
+            kl[j, at, :] = keys
+            vl[j, at, :] = values
 
     for i in (3, 4, 5):
         loads[i].wait()
@@ -197,71 +216,82 @@
             def _():
                 qa[me_r] = q_s[rows_of(to, CH), :]
 
+    def attend(q, k, v, extra, m_ref, o_ref, fresh):
+        vs = (v * first + second, v * second + first)
+        scores = [dot_t(q * mask, k) for mask in (first, second)]
+        for h, s in enumerate(scores):
+            if extra is not None:
+                s = extra(s)
+            m_new = jnp.max(s, axis=1, keepdims=True)
+            if fresh:
+                m_new = jnp.broadcast_to(m_new, (256, WIDE))
+            else:
+                m_old = m_ref[h]
+                m_new = jnp.maximum(m_old, m_new)
+            wide = jnp.concatenate([m_new] * (s.shape[1] // WIDE), axis=1)
+            o = dot(jnp.exp(s - wide).astype(BF16), vs[h])
+            o_ref[h] = o if fresh else o_ref[h] * jnp.exp(m_old - m_new) + o
+            m_ref[h] = m_new
+
+    def attend_end(m_ref, o_ref):
+        low = lax.broadcasted_iota(jnp.int32, (256, WIDE), 1) < 64
+        total = pltpu.roll(jnp.where(low, o_ref[1], o_ref[0]), 64, 1)
+        return jnp.where(low, m_ref[0], m_ref[1]), total, jnp.where(low, o_ref[0], o_ref[1])
+
+    m_s[...] = jnp.full(m_s.shape, LOW, F32)
+    o_s[...] = jnp.zeros(o_s.shape, F32)
+
+    def attend_short(b):
+        attend(
+            q_s[rows_of(b, 256), :], k_s[:SHORT, :], v_s[:SHORT, :], lambda s: s + bias[0:1, :],
+            m_s.at[b], o_s.at[b], False,
+        )
+
+    def attend_new(b):
+        at = slice(SHORT, SHORT + 256 * (b + 1))
+        causal = jnp.where(col256 <= row256, 0.0, LOW)
+
+        def extra(s):
+            last = s[:, 256 * b :] + causal
+            return jnp.concatenate([s[:, : 256 * b], last], axis=1) if b else last
+
+        attend(q_s[b * 256 : (b + 1) * 256, :], k_s[at, :], v_s[at, :], extra, m_s.at[b], o_s.at[b], False)
+
+    def attend_local_end(b):
+        m, total, o = attend_end(m_s.at[b], o_s.at[b])
+        m_l[rows_of(b, 256), :] = m
+        l_l[rows_of(b, 256), :] = total
+        o_l[rows_of(b, 256), :] = o
+
     project(me_t)
     gather_sibling(hid, s_hr, 0)
     project(y * 2 + 1 - c)
-    unweave_long(0)
-    for step, yy in ((1, yl), (2, yr), (3, yf)):
-        sent += gather_step(hid, s_hs, s_hr, step)
-        project(yy * 2 + c)
-    for step, yy in ((1, yl), (2, yr), (3, yf)):
-        gather_sibling(hid, s_hr, step)
-        project(yy * 2 + 1 - c)
+    attend_short(y)
+    gather_forward(hid, s_hs, s_hr)
+    gather_share(hid, s_hs, s_hr, 1)
+    project(yl * 2 + c)
+    gather_share(hid, s_hs, s_hr, 2)
+    project(yr * 2 + c)
+    gather_sibling(hid, s_hr, 1)
+    project(yl * 2 + 1 - c)
+    x_forward(0)
+    gather_share(hid, s_hs, s_hr, 3)
+    project(yf * 2 + c)
+    gather_sibling(hid, s_hr, 2)
+    project(yr * 2 + 1 - c)
+    gather_sibling(hid, s_hr, 3)
+    project(yf * 2 + 1 - c)
 
     for i in (6, 7, 8, 9):
         loads[i].wait()
-    sent += gather_start(wo, s_ws, s_wr)
-    swap = [
-        remote(w1.at[c], w1.at[c], s_es.at[0], s_er.at[0], sibling),
-        remote(w2.at[c], w2.at[c], s_es.at[1], s_er.at[1], sibling),
-        remote(b1.at[c], b1.at[c], s_es.at[2], s_er.at[2], sibling),
-    ]
-    for copy in swap:
-        copy.start()
-    sent += swap
-
-    def attend_init():
-        m_st[...] = jnp.full(m_st.shape, LOW, F32)
-        o_st[...] = jnp.zeros(o_st.shape, F32)
-
-    def attend_step(q, k, v, extra):
-        vs = (v * first + second, v * second + first)
-        for h, mask in enumerate((first, second)):
-            s = dot_t(q * mask, k)
-            if extra is not None:
-                s = s + extra
-            m_old = m_st[h]
-            m_new = jnp.maximum(m_old, jnp.max(s, axis=1, keepdims=True))
-            wide = jnp.concatenate([m_new] * (s.shape[1] // WIDE), axis=1)
-            p = jnp.exp(s - wide).astype(BF16)
-            o_st[h] = o_st[h] * jnp.exp(m_old - m_new) + dot(p, vs[h])
-            m_st[h] = m_new
-
-    def attend_end():
-        low = lax.broadcasted_iota(jnp.int32, (256, WIDE), 1) < 64
-        total = pltpu.roll(jnp.where(low, o_st[1], o_st[0]), 64, 1)
-        return jnp.where(low, m_st[0], m_st[1]), total, jnp.where(low, o_st[0], o_st[1])
-
-    def attend_local(b):
-        q = q_s[rows_of(b, 256), :]
-        attend_init()
-
-        @pl.loop(0, 3)
-        def _(i):
-            at = rows_of(i, 512)
-            attend_step(q, k_s[at, :], v_s[at, :], bias[0:1, at])
-
-        @pl.loop(0, b)
-        def _(i):
-            at = pl.ds(pl.multiple_of(SHORT + i * 256, 256), 256)
-            attend_step(q, k_s[at, :], v_s[at, :], None)
-
-        at = pl.ds(pl.multiple_of(SHORT + b * 256, 256), 256)
-        attend_step(q, k_s[at, :], v_s[at, :], jnp.where(col256 <= row256, 0.0, LOW))
-        m, total, o = attend_end()
-        m_l[rows_of(b, 256), :] = m
-        l_l[rows_of(b, 256), :] = total
-        o_l[rows_of(b, 256), :] = o
+    gather_start(wo, s_ws, s_wr)
+    begin(w1.at[c], w1.at[c], s_es.at[0], s_er.at[0], sibling)
+    begin(w2.at[c], w2.at[c], s_es.at[1], s_er.at[1], sibling)
+    begin(b1.at[c], b1.at[c], s_es.at[2], s_er.at[2], sibling)
+    x_forward(1)
+    for j in range(NLONG):
+        unweave_long(j, 0)
+    attend_short(yl)
 
     lane32 = lax.broadcasted_iota(jnp.int32, (CH, WIDE), 1) % 64
     diagonal = jnp.where(lane32 == lax.broadcasted_iota(jnp.int32, (CH, WIDE), 0), 1.0, 0.0)
@@ -288,10 +318,6 @@
             lse = term if lse is None else lse + term
         return lse
 
-    @pl.loop(0, 2)
-    def _(b):
-        attend_local(b)
-
     await_bytes(qa.at[pl.ds(0, NREQ - 1)], s_qar)
     for j in range(NLONG):
         sel[j] = qa[owner[j]]
@@ -302,39 +328,38 @@
         to = x * NZ + (z + d) % NZ
         remote(sel, qz.at[d], s_qzs, s_qzr, (to, me_t)).start()
 
-    await_bytes(long_raw.at[1], s_xr.at[0])
-    half = pl.ds(0, SHORT)
-    copy = remote(long_raw.at[1, half], long_raw.at[3, half], s_xs.at[2], s_xr.at[2], x_right)
-    copy.start()
-    sent.append(copy)
-    await_bytes(long_raw.at[2], s_xr.at[1])
-    half = pl.ds(SHORT, SHORT)
-    copy = remote(long_raw.at[2, half], long_raw.at[3, half], s_xs.at[3], s_xr.at[3], x_left)
-    copy.start()
-    sent.append(copy)
-    for step in (1, 2):
-        sent += gather_step(wo, s_ws, s_wr, step)
-    unweave_long(1)
-    unweave_long(2)
-
-    attend_local(2)
-    sent += gather_step(wo, s_ws, s_wr, 3)
-
-    await_bytes(long_raw.at[3, pl.ds(0, SHORT)], s_xr.at[2])
-    await_bytes(long_raw.at[3, pl.ds(SHORT, SHORT)], s_xr.at[3])
-    unweave_long(3)
+    x_send(2)
+
+    @pl.loop(0, 4)
+    def _(g):
+        for i in range(2):
+            t = g * 2 + i
+            at = pl.ds(pl.multiple_of(SHORT + t * 128, 128), 128)
+            both = jnp.concatenate([k_s[at, :], v_s[at, :]], axis=0)
+            kvout[rows_of(t, 256), :] = dot(weave[...], both).astype(BF16)
+
+    out_copy = pltpu.make_async_copy(kvout, newkv_hbm, s_out.at[0])
+    out_copy.start()
+    gather_forward(wo, s_ws, s_wr)
+    attend_new(0)
+    attend_new(1)
+    for j in range(2):
+        unweave_long(j, 1)
+        unweave_long(j, 2)
+    x_forward(2)
+    unweave_long(2, 1)
+    unweave_long(2, 2)
+    for step in (1, 2, 3):
+        gather_share(wo, s_ws, s_wr, step)
     await_bytes(qz.at[pl.ds(1, NZ - 1)], s_qzr)
 
     @pl.loop(0, NLONG)
     def _(j):
-        q = qz[:, j].reshape(256, WIDE)
-        attend_init()
-
-        @pl.loop(0, NX)
-        def _(i):
-            attend_step(q, kl[j * 4 + i], vl[j * 4 + i], None)
-
-        m, total, o = attend_end()
+        for half in range(2):
+            await_bytes(long_raw.at[3, x_rows(j, half)], s_xr.at[4 * j + 2 + half])
+        unweave_long(j, 3)
+        attend(qz[:, j].reshape(256, WIDE), kl[j], vl[j], None, m_g, o_g, True)
+        m, total, o = attend_end(m_g, o_g)
         lse = m + jnp.log(total)
         o = (o / total).astype(BF16)
         for d in range(NZ):
@@ -348,7 +373,8 @@
             to = x * NZ + (z + NZ - d) % NZ
             remote(ps.at[j, d], pr.at[j, d], s_ps.at[j], s_pr.at[j], (to, me_t)).start()
 
-    attend_local(3)
+    attend_short(yr)
+    attend_new(2)
 
     @pl.loop(0, NLONG)
     def _(j):
@@ -383,16 +409,10 @@
             rs[r] = message
             remote(rs.at[r], rr.at[me_r], s_rs, s_rr, (r, me_t)).start()
 
-    @pl.loop(0, 4)
-    def _(g):
-        for i in range(2):
-            t = g * 2 + i
-            at = pl.ds(pl.multiple_of(SHORT + t * 128, 128), 128)
-            both = jnp.concatenate([k_s[at, :], v_s[at, :]], axis=0)
-            kvout[rows_of(t, 256), :] = dot(weave[...], both).astype(BF16)
-
-    out_copy = pltpu.make_async_copy(kvout, newkv_hbm, s_out.at[0])
-    out_copy.start()
+    attend_short(yf)
+    attend_new(3)
+    for b in range(4):
+        attend_local_end(b)
 
     await_bytes(rr.at[pl.ds(0, NREQ - 1)], s_rr)
 
@@ -432,13 +452,10 @@
 
     nrm[0] = norm(hid[me_t].astype(F32) + attended, 0)
 
-    copies = [
-        remote(nrm.at[0], nrm.at[1], s_ns.at[0], s_nr.at[0], right),
-        remote(nrm.at[0], nrm.at[2], s_ns.at[1], s_nr.at[1], left),
-    ]
-    for copy in copies:
-        copy.start()
-    sent += copies
+    begin(nrm.at[0, top_half], nrm.at[1, top_half], s_ns.at[0], s_nr.at[0], right)
+    begin(nrm.at[0, low_half], nrm.at[2, low_half], s_ns.at[2], s_nr.at[2], left)
+    begin(nrm.at[0, low_half], nrm.at[1, low_half], s_ns.at[1], s_nr.at[1], right)
+    begin(nrm.at[0, top_half], nrm.at[2, top_half], s_ns.at[3], s_nr.at[3], left)
     await_bytes(w1.at[1 - c], s_er.at[0])
     await_bytes(w2.at[1 - c], s_er.at[1])
     await_bytes(b1.at[1 - c], s_er.at[2])
@@ -453,32 +470,28 @@
             total = term if total is None else total + term
         return total
 
-    def start(*args):
-        copy = remote(*args)
-        copy.start()
-        sent.append(copy)
-
-    top_half, low_half = pl.ds(0, 64), pl.ds(64, 64)
     own_sum[...] = feed(0)
-    await_bytes(nrm.at[1], s_nr.at[0])
-    start(nrm.at[1, top_half], nrm.at[3, top_half], s_ns.at[2], s_nr.at[2], right)
-    await_bytes(nrm.at[2], s_nr.at[1])
-    start(nrm.at[2, low_half], nrm.at[3, low_half], s_ns.at[3], s_nr.at[3], left)
+    await_bytes(nrm.at[1, top_half], s_nr.at[0])
+    begin(nrm.at[1, top_half], nrm.at[3, top_half], s_ns.at[4], s_nr.at[4], right)
+    await_bytes(nrm.at[2, low_half], s_nr.at[2])
+    begin(nrm.at[2, low_half], nrm.at[3, low_half], s_ns.at[5], s_nr.at[5], left)
+    await_bytes(nrm.at[1, low_half], s_nr.at[1])
     part[1] = feed(1).astype(BF16)
-    start(part.at[1, top_half], fr.at[top_half], s_fs.at[0], s_fr.at[0], left)
+    begin(part.at[1, top_half], fr.at[top_half], s_fs.at[0], s_fr.at[0], left)
+    await_bytes(nrm.at[2, top_half], s_nr.at[3])
     part[2] = feed(2).astype(BF16)
-    start(part.at[2, low_half], fl.at[low_half], s_fs.at[1], s_fr.at[1], right)
-    await_bytes(nrm.at[3, top_half], s_nr.at[2])
-    await_bytes(nrm.at[3, low_half], s_nr.at[3])
+    begin(part.at[2, low_half], fl.at[low_half], s_fs.at[1], s_fr.at[1], right)
+    await_bytes(nrm.at[3, top_half], s_nr.at[4])
+    await_bytes(nrm.at[3, low_half], s_nr.at[5])
     part[3] = feed(3).astype(BF16)
-    start(part.at[3, top_half], ra, s_fs.at[2], s_fr.at[2], right)
-    start(part.at[3, low_half], rb, s_fs.at[3], s_fr.at[3], left)
+    begin(part.at[3, top_half], ra, s_fs.at[2], s_fr.at[2], right)
+    begin(part.at[3, low_half], rb, s_fs.at[3], s_fr.at[3], left)
     await_bytes(ra, s_fr.at[2])
     part[2, 0:64] = (part[2, 0:64].astype(F32) + ra[...].astype(F32)).astype(BF16)
-    start(part.at[2, top_half], fl.at[top_half], s_fs.at[4], s_fr.at[4], right)
+    begin(part.at[2, top_half], fl.at[top_half], s_fs.at[4], s_fr.at[4], right)
     await_bytes(rb, s_fr.at[3])
     part[1, 64:128] = (part[1, 64:128].astype(F32) + rb[...].astype(F32)).astype(BF16)
-    start(part.at[1, low_half], fr.at[low_half], s_fs.at[5], s_fr.at[5], left)
+    begin(part.at[1, low_half], fr.at[low_half], s_fs.at[5], s_fr.at[5], left)
     await_bytes(fr.at[top_half], s_fr.at[0])
     await_bytes(fl.at[low_half], s_fr.at[1])
     await_bytes(fl.at[top_half], s_fr.at[4])
@@ -527,14 +540,16 @@
             V((SPAN, WIDE), BF16),
             V((SHORT + SPAN, WIDE), BF16),
             V((SHORT + SPAN, WIDE), BF16),
-            V((NLONG * NX, LSEG, WIDE), BF16),
-            V((NLONG * NX, LSEG, WIDE), BF16),
+            V((NLONG, NX * LSEG, WIDE), BF16),
+            V((NLONG, NX * LSEG, WIDE), BF16),
             V((NREQ, CH, WIDE), BF16),
             V((NLONG, CH, WIDE), BF16),
             V((NZ, NLONG, CH, WIDE), BF16),
             V((8, SHORT), F32),
             V((256, 256), BF16),
             V((256, 256), BF16),
+            V((4, 2, 256, WIDE), F32),
+            V((4, 2, 256, WIDE), F32),
             V((2, 256, WIDE), F32),
             V((2, 256, WIDE), F32),
             V((SPAN, WIDE), F32),
@@ -555,8 +570,8 @@
             V((128, D), BF16),
             V((128, D), BF16),
             V((2 * SPAN, WIDE), BF16),
-            S((10,)), S((8,)), S((8,)), S((8,)), S((8,)), S((4,)), S((4,)), S((3,)), S((3,)),
-            S, S, S, S, S((3,)), S((3,)), S, S, S, S, S((4,)), S((4,)), S((6,)), S((6,)), S((1,)),
+            S((10,)), S((12,)), S((12,)), S((12,)), S((12,)), S((12,)), S((12,)), S((3,)), S((3,)),
+            S, S, S, S, S((3,)), S((3,)), S, S, S, S, S((6,)), S((6,)), S((6,)), S((6,)), S((1,)),
         ],
         compiler_params=pltpu.CompilerParams(
             collective_id=0, has_side_effects=True, vmem_limit_bytes=56 * 1024 * 1024

time: 106 us -> 96.9 us (0.914)
  Pallas kernels: 102 us -> 93 us
    pallas_call x1, Pallas kernels: 102 us -> 93 us  [body(): pl.pallas_call(kernel, out_shape=(jax.ShapeDtypeStruct((128, D), BF16), j...]
where the time goes in v2:
time: 96.9 us; the launch traced here: 96.8 us
  Pallas kernels  93 us (96%)
  local copies, waits for them, and re-layouts  2.52 us (3%)
  between operations  1.3 us (1%)
    pallas_call x1, Pallas kernels, body(): pl.pallas_call(kernel, out_shape=(jax.ShapeDtypeStruct((128, D), BF16), j...  93 us
    unnamed x4, local copies, waits for them, and re-layouts  2.52 us

profile of v2, /device:TPU:6, one launch (start us, length us, event | category | flops | bytes accessed | tf_op | source)
XLA Modules:
  0.0 96.8 jit_solution(14225055254443698418)
XLA Ops:
  1.3 93.0 %shard_map.158 = (bf16[128,1024]{1,0:T(8,128)(2,1)}, bf16[2048,128]{1,0:T(8,128)(2,1)}) custom-call(bf16[128,1024]{1,0:T(8,128)(2,1)} %bitcast.11, bf16[3072,128]{1,0:T(8,128)(2,1)} %bitcast.8, bf16[3072,128]{1,0:T(8,128)(2,1)} %bitcast.9, s32[1]{0:T(128)S(6)} %copy.19.short_len, s32[3]{0:T(128)} %owner.1, bf16[3,1024,128]{2,1,0:T(8,128)(2,1)} %wqkv_hbm.1, ...), custom_call_target="tpu_custom_call" | custom-call | tf_op jit(solution)/shard_map/pallas_call | solution.py:521
  94.3 0.0 copy-start
  94.3 1.7 %copy.20 = bf16[1,128,1024]{2,1,0:T(8,128)(2,1)} copy(bf16[1,128,1024]{2,1,0:T(8,128)(2,1)} %bitcast.12) | data formatting | bytes 524288
  96.0 0.0 copy-done
  96.0 0.8 copy.21
Async XLA Ops:
  94.3 1.7 %copy-start = (bf16[2048,128]{1,0:T(8,128)(2,1)S(1)}, bf16[2048,128]{1,0:T(8,128)(2,1)}, u32[]{:S(2)}) copy-start(bf16[2048,128]{1,0:T(8,128)(2,1)} %get-tuple-element.5) | copy-start | bytes 1572868

commit v3 on v2

--- a/solution.py
+++ b/solution.py
@@ -15,8 +15,8 @@
 SPAN, D, WIDE = 1024, 1024, 128
 SHORT, LSEG, NLONG = 1536, 512, 3
 CH = 32
-MSG = 48
 FFH = 512
+NP = 4
 
 
 def dot(a, b):
@@ -36,7 +36,7 @@
     win_hbm, bin_hbm, wdown_hbm, b_down, gain, offset,
     out_ref, newkv_hbm,
     hid, wq, short_raw, long_raw, wo, w1, w2, b1, q_s, k_s, v_s, kl, vl, qa, sel, qz, bias,
-    spread, weave, m_s, o_s, m_g, o_g, m_l, l_l, o_l, ps, pr, merged, rs, rr, ctx, cr, nrm, part,
+    spread, weave, m_s, o_s, m_g, o_g, m_l, l_l, o_l, ps, pr, pst, prt, merged, merged_t, rs, rr, rst, rrt, ctx, cr, nrm, part,
     own_sum, ra, rb, fl, fr, kvout,
     s_loc, s_hs, s_hr, s_ws, s_wr, s_xs, s_xr, s_es, s_er, s_qas, s_qar, s_qzs, s_qzr,
     s_ps, s_pr, s_rs, s_rr, s_cs, s_cr, s_ns, s_nr, s_fs, s_fr, s_out,
@@ -295,26 +295,19 @@
 
     lane32 = lax.broadcasted_iota(jnp.int32, (CH, WIDE), 1) % 64
     diagonal = jnp.where(lane32 == lax.broadcasted_iota(jnp.int32, (CH, WIDE), 0), 1.0, 0.0)
-    tile_row = lax.broadcasted_iota(jnp.int32, (16, WIDE), 0)
     side_r = lax.broadcasted_iota(jnp.int32, (WIDE, WIDE), 0) // 64
     side_c = lax.broadcasted_iota(jnp.int32, (WIDE, WIDE), 1) // 64
     sides = jnp.where(side_r == side_c, 1.0, 0.0).astype(BF16)
 
     def pack_stats(lse):
-        row = jnp.sum(lse * diagonal, axis=0, keepdims=True)
-        hi = row.astype(BF16).astype(F32)
-        mid = (row - hi).astype(BF16).astype(F32)
-        lo = row - hi - mid
-        tile = jnp.where(tile_row == 0, hi, jnp.where(tile_row == 1, mid, jnp.where(tile_row == 2, lo, 0.0)))
-        return tile.astype(BF16)
-
-    def unpack_stats(tiles):
-        n = tiles.shape[0]
-        tiles = tiles.astype(F32)
-        lse = None
-        for i in range(3):
-            spread_out = tiles[:, i : i + 1, :] * diagonal[None]
-            term = dot(spread_out.reshape(n * CH, WIDE).astype(BF16), sides)
+        return jnp.sum(lse * diagonal, axis=0, keepdims=True)
+
+    def unpack_stats(rows):
+        n, rest, lse = rows.shape[0], rows, None
+        for _ in range(3):
+            piece = rest.astype(BF16).astype(F32)
+            rest = rest - piece
+            term = dot((piece * diagonal[None]).reshape(n * CH, WIDE).astype(BF16), sides)
             lse = term if lse is None else lse + term
         return lse
 
@@ -364,14 +357,15 @@
         o = (o / total).astype(BF16)
         for d in range(NZ):
             at = slice(d * CH, (d + 1) * CH)
-            dst = pr if d == 0 else ps
-            dst[j, d, 0:CH] = o[at]
-            dst[j, d, CH:MSG] = pack_stats(lse[at])
+            dst, dst_stats = (pr, prt) if d == 0 else (ps, pst)
+            dst[j, d] = o[at]
+            dst_stats[j, d] = pack_stats(lse[at])
 
         @pl.loop(1, NZ)
         def _(d):
-            to = x * NZ + (z + NZ - d) % NZ
-            remote(ps.at[j, d], pr.at[j, d], s_ps.at[j], s_pr.at[j], (to, me_t)).start()
+            to = (x * NZ + (z + NZ - d) % NZ, me_t)
+            remote(ps.at[j, d], pr.at[j, d], s_ps.at[j], s_pr.at[j], to).start()
+            remote(pst.at[j, d], prt.at[j, d], s_ps.at[3 + j], s_pr.at[3 + j], to).start()
 
     attend_short(yr)
     attend_new(2)
@@ -379,49 +373,49 @@
     @pl.loop(0, NLONG)
     def _(j):
         await_bytes(pr.at[j, pl.ds(1, NZ - 1)], s_pr.at[j])
-        lse = unpack_stats(pr[j, :, CH:MSG]).reshape(NZ, CH, WIDE)
+        await_bytes(prt.at[j, pl.ds(1, NZ - 1)], s_pr.at[3 + j])
+        lse = unpack_stats(prt[j]).reshape(NZ, CH, WIDE)
         top = jnp.max(lse, axis=0, keepdims=True)
         w = jnp.exp(lse - top)
         total = jnp.sum(w, axis=0)
-        o = jnp.sum(w * pr[j, :, 0:CH].astype(F32), axis=0) / total
-        merged[j, 0:CH] = o
-        merged[j, CH:MSG] = pack_stats(top[0] + jnp.log(total)).astype(F32)
-
-    msg_row = lax.broadcasted_iota(jnp.int32, (MSG, WIDE), 0)
-    empty = jnp.where(msg_row == CH, LOW, 0.0)
+        merged[j] = jnp.sum(w * pr[j].astype(F32), axis=0) / total
+        merged_t[j] = pack_stats(top[0] + jnp.log(total))
 
     @pl.loop(0, NREQ)
     def _(r):
-        value, rest = None, 1.0
+        value, stats, rest = None, None, 1.0
         for j in range(NLONG):
             mine = jnp.where(owner[j] == r, 1.0, 0.0)
-            term = merged[j] * mine
-            value = term if value is None else value + term
+            value = merged[j] * mine if j == 0 else value + merged[j] * mine
+            stats = merged_t[j] * mine if j == 0 else stats + merged_t[j] * mine
             rest = rest - mine
-        message = (value + empty * rest).astype(BF16)
+        value, stats = value.astype(BF16), stats + LOW * rest
 
         @pl.when(r == me_r)
         def _():
-            rr[me_r] = message
+            rr[me_r] = value
+            rrt[me_r] = stats
 
         @pl.when(r != me_r)
         def _():
-            rs[r] = message
-            remote(rs.at[r], rr.at[me_r], s_rs, s_rr, (r, me_t)).start()
+            rs[r] = value
+            rst[r] = stats
+            remote(rs.at[r], rr.at[me_r], s_rs.at[0], s_rr.at[0], (r, me_t)).start()
+            remote(rst.at[r], rrt.at[me_r], s_rs.at[1], s_rr.at[1], (r, me_t)).start()
 
     attend_short(yf)
     attend_new(3)
     for b in range(4):
         attend_local_end(b)
 
-    await_bytes(rr.at[pl.ds(0, NREQ - 1)], s_rr)
+    await_bytes(rr.at[pl.ds(0, NREQ - 1)], s_rr.at[0])
+    await_bytes(rrt.at[pl.ds(0, NREQ - 1)], s_rr.at[1])
 
     @pl.loop(0, 4)
     def _(b):
         at = rows_of(b, 256)
-        msgs = rr[pl.ds(b * 8, 8)]
-        lse = unpack_stats(msgs[:, CH:MSG])
-        o = msgs[:, 0:CH].astype(F32).reshape(256, WIDE)
+        lse = unpack_stats(rrt[pl.ds(b * 8, 8)])
+        o = rr[pl.ds(b * 8, 8)].astype(F32).reshape(256, WIDE)
         m = m_l[at, :]
         top = jnp.maximum(m, lse)
         a, w = jnp.exp(m - top), jnp.exp(lse - top)
@@ -469,6 +463,9 @@
             term = dot(u, w2[i])
             total = term if total is None else total + term
         return total
+
+    def piece(i):
+        return pl.ds(i * (D // NP), D // NP)
 
     own_sum[...] = feed(0)
     await_bytes(nrm.at[1, top_half], s_nr.at[0])
@@ -484,18 +481,22 @@
     await_bytes(nrm.at[3, top_half], s_nr.at[4])
     await_bytes(nrm.at[3, low_half], s_nr.at[5])
     part[3] = feed(3).astype(BF16)
-    begin(part.at[3, top_half], ra, s_fs.at[2], s_fr.at[2], right)
-    begin(part.at[3, low_half], rb, s_fs.at[3], s_fr.at[3], left)
-    await_bytes(ra, s_fr.at[2])
-    part[2, 0:64] = (part[2, 0:64].astype(F32) + ra[...].astype(F32)).astype(BF16)
-    begin(part.at[2, top_half], fl.at[top_half], s_fs.at[4], s_fr.at[4], right)
-    await_bytes(rb, s_fr.at[3])
-    part[1, 64:128] = (part[1, 64:128].astype(F32) + rb[...].astype(F32)).astype(BF16)
-    begin(part.at[1, low_half], fr.at[low_half], s_fs.at[5], s_fr.at[5], left)
+    for i in range(NP):
+        begin(part.at[3, top_half, piece(i)], ra.at[:, piece(i)], s_fs.at[2 + 4 * i], s_fr.at[2 + 4 * i], right)
+        begin(part.at[3, low_half, piece(i)], rb.at[:, piece(i)], s_fs.at[3 + 4 * i], s_fr.at[3 + 4 * i], left)
+    for i in range(NP):
+        at = piece(i)
+        await_bytes(ra.at[:, at], s_fr.at[2 + 4 * i])
+        part[2, 0:64, at] = (part[2, 0:64, at].astype(F32) + ra[:, at].astype(F32)).astype(BF16)
+        begin(part.at[2, top_half, at], fl.at[top_half, at], s_fs.at[4 + 4 * i], s_fr.at[4 + 4 * i], right)
+        await_bytes(rb.at[:, at], s_fr.at[3 + 4 * i])
+        part[1, 64:128, at] = (part[1, 64:128, at].astype(F32) + rb[:, at].astype(F32)).astype(BF16)
+        begin(part.at[1, low_half, at], fr.at[low_half, at], s_fs.at[5 + 4 * i], s_fr.at[5 + 4 * i], left)
     await_bytes(fr.at[top_half], s_fr.at[0])
     await_bytes(fl.at[low_half], s_fr.at[1])
-    await_bytes(fl.at[top_half], s_fr.at[4])
-    await_bytes(fr.at[low_half], s_fr.at[5])
+    for i in range(NP):
+        await_bytes(fl.at[top_half, piece(i)], s_fr.at[4 + 4 * i])
+        await_bytes(fr.at[low_half, piece(i)], s_fr.at[5 + 4 * i])
     mixed = own_sum[...] + fl[...].astype(F32) + fr[...].astype(F32) + b_down[...]
     out_ref[...] = norm(nrm[0].astype(F32) + mixed, 1)
 
@@ -505,7 +506,9 @@
     await_bytes(qz.at[pl.ds(1, NZ - 1)], s_qzs)
     for j in range(NLONG):
         await_bytes(pr.at[j, pl.ds(1, NZ - 1)], s_ps.at[j])
-    await_bytes(rr.at[pl.ds(0, NREQ - 1)], s_rs)
+        await_bytes(prt.at[j, pl.ds(1, NZ - 1)], s_ps.at[3 + j])
+    await_bytes(rr.at[pl.ds(0, NREQ - 1)], s_rs.at[0])
+    await_bytes(rrt.at[pl.ds(0, NREQ - 1)], s_rs.at[1])
     await_bytes(cr.at[pl.ds(0, NTP - 1)], s_cs)
     out_copy.wait()
 
@@ -555,11 +558,16 @@
             V((SPAN, WIDE), F32),
             V((SPAN, WIDE), F32),
             V((SPAN, WIDE), F32),
-            V((NLONG, NZ, MSG, WIDE), BF16),
-            V((NLONG, NZ, MSG, WIDE), BF16),
-            V((NLONG, MSG, WIDE), F32),
-            V((NREQ, MSG, WIDE), BF16),
-            V((NREQ, MSG, WIDE), BF16),
+            V((NLONG, NZ, CH, WIDE), BF16),
+            V((NLONG, NZ, CH, WIDE), BF16),
+            V((NLONG, NZ, 1, WIDE), F32),
+            V((NLONG, NZ, 1, WIDE), F32),
+            V((NLONG, CH, WIDE), F32),
+            V((NLONG, 1, WIDE), F32),
+            V((NREQ, CH, WIDE), BF16),
+            V((NREQ, CH, WIDE), BF16),
+            V((NREQ, 1, WIDE), F32),
+            V((NREQ, 1, WIDE), F32),
             V((SPAN, WIDE), BF16),
             V((NTP, 128, WIDE), BF16),
             V((NY, 128, D), BF16),
@@ -571,7 +579,8 @@
             V((128, D), BF16),
             V((2 * SPAN, WIDE), BF16),
             S((10,)), S((12,)), S((12,)), S((12,)), S((12,)), S((12,)), S((12,)), S((3,)), S((3,)),
-            S, S, S, S, S((3,)), S((3,)), S, S, S, S, S((6,)), S((6,)), S((6,)), S((6,)), S((1,)),
+            S, S, S, S, S((6,)), S((6,)), S((2,)), S((2,)), S, S, S((6,)), S((6,)),
+            S((2 + 4 * NP,)), S((2 + 4 * NP,)), S((1,)),
         ],
         compiler_params=pltpu.CompilerParams(
             collective_id=0, has_side_effects=True, vmem_limit_bytes=56 * 1024 * 1024

time: 96.9 us -> 94.3 us (0.973)
  Pallas kernels: 93 us -> 90.4 us
    pallas_call x1, Pallas kernels: 93 us -> 90.4 us  [body(): pl.pallas_call(kernel, out_shape=(jax.ShapeDtypeStruct((128, D), BF16), j...]
where the time goes in v3:
time: 94.3 us; the launch traced here: 94.2 us
  Pallas kernels  90.4 us (96%)
  local copies, waits for them, and re-layouts  2.52 us (3%)
  between operations  1.3 us (1%)
    pallas_call x1, Pallas kernels, body(): pl.pallas_call(kernel, out_shape=(jax.ShapeDtypeStruct((128, D), BF16), j...  90.4 us
    unnamed x4, local copies, waits for them, and re-layouts  2.52 us

profile of v3, /device:TPU:6, one launch (start us, length us, event | category | flops | bytes accessed | tf_op | source)
XLA Modules:
  0.0 94.2 jit_solution(13516364897918560485)
XLA Ops:
  1.3 90.4 %shard_map.158 = (bf16[128,1024]{1,0:T(8,128)(2,1)}, bf16[2048,128]{1,0:T(8,128)(2,1)}) custom-call(bf16[128,1024]{1,0:T(8,128)(2,1)} %bitcast.11, bf16[3072,128]{1,0:T(8,128)(2,1)} %bitcast.8, bf16[3072,128]{1,0:T(8,128)(2,1)} %bitcast.9, s32[1]{0:T(128)S(6)} %copy.19.short_len, s32[3]{0:T(128)} %owner.1, bf16[3,1024,128]{2,1,0:T(8,128)(2,1)} %wqkv_hbm.1, ...), custom_call_target="tpu_custom_call" | custom-call | tf_op jit(solution)/shard_map/pallas_call | solution.py:524
  91.6 0.0 copy-start
  91.7 1.7 %copy.20 = bf16[1,128,1024]{2,1,0:T(8,128)(2,1)} copy(bf16[1,128,1024]{2,1,0:T(8,128)(2,1)} %bitcast.12) | data formatting | bytes 524288
  93.4 0.0 copy-done
  93.4 0.8 copy.21
Async XLA Ops:
  91.6 1.7 %copy-start = (bf16[2048,128]{1,0:T(8,128)(2,1)S(1)}, bf16[2048,128]{1,0:T(8,128)(2,1)}, u32[]{:S(2)}) copy-start(bf16[2048,128]{1,0:T(8,128)(2,1)} %get-tuple-element.5) | copy-start | bytes 1572868

commit v4 on v3

--- a/solution.py
+++ b/solution.py
@@ -206,15 +206,15 @@
 
         @pl.loop(0, 4)
         def _(i):
-            to = 4 * t + i
+            to, at = i * NZ + t, rows_of(4 * t + i, CH)
 
             @pl.when(to != me_r)
             def _():
-                remote(q_s.at[rows_of(to, CH), :], qa.at[me_r], s_qas, s_qar, (to, me_t)).start()
+                remote(q_s.at[at, :], qa.at[me_r], s_qas, s_qar, (to, me_t)).start()
 
             @pl.when(to == me_r)
             def _():
-                qa[me_r] = q_s[rows_of(to, CH), :]
+                qa[me_r] = q_s[at, :]
 
     def attend(q, k, v, extra, m_ref, o_ref, fresh):
         vs = (v * first + second, v * second + first)
@@ -381,8 +381,11 @@
         merged[j] = jnp.sum(w * pr[j].astype(F32), axis=0) / total
         merged_t[j] = pack_stats(top[0] + jnp.log(total))
 
+    chunk = z * NX + x
+
     @pl.loop(0, NREQ)
-    def _(r):
+    def _(d):
+        r = (me_r + 1 + d) % NREQ
         value, stats, rest = None, None, 1.0
         for j in range(NLONG):
             mine = jnp.where(owner[j] == r, 1.0, 0.0)
@@ -393,15 +396,15 @@
 
         @pl.when(r == me_r)
         def _():
-            rr[me_r] = value
-            rrt[me_r] = stats
+            rr[chunk] = value
+            rrt[chunk] = stats
 
         @pl.when(r != me_r)
         def _():
             rs[r] = value
             rst[r] = stats
-            remote(rs.at[r], rr.at[me_r], s_rs.at[0], s_rr.at[0], (r, me_t)).start()
-            remote(rst.at[r], rrt.at[me_r], s_rs.at[1], s_rr.at[1], (r, me_t)).start()
+            remote(rs.at[r], rr.at[chunk], s_rs.at[0], s_rr.at[0], (r, me_t)).start()
+            remote(rst.at[r], rrt.at[chunk], s_rs.at[1], s_rr.at[1], (r, me_t)).start()
 
     attend_short(yf)
     attend_new(3)
@@ -412,7 +415,8 @@
     await_bytes(rrt.at[pl.ds(0, NREQ - 1)], s_rr.at[1])
 
     @pl.loop(0, 4)
-    def _(b):
+    def _(n):
+        b = (y + 1 + n) % NY
         at = rows_of(b, 256)
         lse = unpack_stats(rrt[pl.ds(b * 8, 8)])
         o = rr[pl.ds(b * 8, 8)].astype(F32).reshape(256, WIDE)
@@ -435,9 +439,8 @@
     for step in range(4):
         gather_sibling(wo, s_wr, step)
     await_bytes(cr.at[pl.ds(0, NTP - 1)], s_cr)
-    attended = b_out[...]
-    for h in range(NTP):
-        attended = attended + dot(cr[h], wo[h])
+    context = jnp.concatenate([cr[h] for h in range(NTP)], axis=1)
+    attended = dot(context, wo[...].reshape(D, D)) + b_out[...]
 
     def norm(rows, which):
         center = rows - jnp.mean(rows, axis=-1, keepdims=True)

time: 94.3 us -> 93.5 us (level)
  Pallas kernels: 90.4 us -> 88.8 us
    pallas_call x1, Pallas kernels: 90.4 us -> 88.8 us  [body(): pl.pallas_call(kernel, out_shape=(jax.ShapeDtypeStruct((128, D), BF16), j...]
where the time goes in v4:
time: 93.5 us; the launch traced here: 92.6 us
  Pallas kernels  88.8 us (95%)
  local copies, waits for them, and re-layouts  2.52 us (3%)
  between operations  1.3 us (1%)
    pallas_call x1, Pallas kernels, body(): pl.pallas_call(kernel, out_shape=(jax.ShapeDtypeStruct((128, D), BF16), j...  88.8 us
    unnamed x4, local copies, waits for them, and re-layouts  2.52 us

profile of v4, /device:TPU:6, one launch (start us, length us, event | category | flops | bytes accessed | tf_op | source)
XLA Modules:
  0.0 92.6 jit_solution(1318859429041294509)
XLA Ops:
  1.3 88.8 %shard_map.158 = (bf16[128,1024]{1,0:T(8,128)(2,1)}, bf16[2048,128]{1,0:T(8,128)(2,1)}) custom-call(bf16[128,1024]{1,0:T(8,128)(2,1)} %bitcast.11, bf16[3072,128]{1,0:T(8,128)(2,1)} %bitcast.8, bf16[3072,128]{1,0:T(8,128)(2,1)} %bitcast.9, s32[1]{0:T(128)S(6)} %copy.19.short_len, s32[3]{0:T(128)} %owner.1, bf16[3,1024,128]{2,1,0:T(8,128)(2,1)} %wqkv_hbm.1, ...), custom_call_target="tpu_custom_call" | custom-call | tf_op jit(solution)/shard_map/pallas_call | solution.py:527
  90.1 0.0 copy-start
  90.1 1.7 %copy.20 = bf16[1,128,1024]{2,1,0:T(8,128)(2,1)} copy(bf16[1,128,1024]{2,1,0:T(8,128)(2,1)} %bitcast.12) | data formatting | bytes 524288
  91.8 0.0 copy-done
  91.8 0.8 copy.21
Async XLA Ops:
  90.1 1.7 %copy-start = (bf16[2048,128]{1,0:T(8,128)(2,1)S(1)}, bf16[2048,128]{1,0:T(8,128)(2,1)}, u32[]{:S(2)}) copy-start(bf16[2048,128]{1,0:T(8,128)(2,1)} %get-tuple-element.5) | copy-start | bytes 1572868
